TPU v7x, 32 devices: a whole 2x2x4 slice. The times are simulated.
32 devices in a mesh: expert: 16 (over z, y, core), hidden: 2 (over x).
Axes of the slice: x: 2, y: 2, z: 4, core: 2. Of those that a mesh axis runs over, the one named last changes fastest.
Arguments:
- tokens: bfloat16 [256, 3584], P(('expert', 'hidden')), may hold values from -6 to 6
- routes: int32 [256, 8], P(('expert', 'hidden')), may hold values from 0 to 15, all different within a row; in each aligned block of 16 rows (0 to 15, 16 to 31, ...) at most 16 rows name the same one
- gate_weights: bfloat16 [256, 8], P(('expert', 'hidden')), may hold values from 0.049804688 to 0.59765625
- w_in: bfloat16 [16, 3584, 1024], P('expert', None, 'hidden'), may hold values from -0.09375 to 0.09375
- w_out: bfloat16 [16, 1024, 3584], P('expert', 'hidden'), may hold values from -0.1875 to 0.1875
Outputs:
- mixed: bfloat16 [256, 3584], P(('expert', 'hidden'))
Inputs may be any that keep to these rules, and one draw needn't show every extreme that they name: `routes`: the 8 experts of a token differ. In each aligned block of 16 tokens no expert is named by more than 16 tokens, a bound that some block reaches.
All inputs are finite; a program needn't handle non-finite values.
Results may differ from a plain program's by a relative error of at most 0.01.
Values may be sent and summed in bfloat16 or wider, within the bound.
A program may use at most 64 MiB of HBM per device.

v0:
```python
import jax
import jax.numpy as jnp
from jax import lax
from jax.sharding import PartitionSpec as P


def per_device(tokens, routes, gate_weights, w_in, w_out):
    group_x, group_routes, group_gates = (
        lax.all_gather(tokens, "hidden", axis=0, tiled=True),
        lax.all_gather(routes, "hidden", axis=0, tiled=True),
        lax.all_gather(gate_weights, "hidden", axis=0, tiled=True),
    )
    group = group_x.shape[0]
    top = group_routes.shape[1]
    experts = w_in.shape[0] * lax.axis_size("expert")
    capacity = min(group, 2 * group * top // experts)
    items = group * top
    expert_ids = group_routes.reshape(items)
    onehot = (expert_ids[:, None] == jnp.arange(experts, dtype=jnp.int32)[None, :]).astype(
        jnp.int32
    )
    before = jnp.cumsum(onehot, axis=0) - onehot
    rank = jnp.sum(before * onehot, axis=1)
    slot = expert_ids * capacity + rank
    token_of_item = jnp.arange(items, dtype=jnp.int32) // top
    match = slot[None, :] == jnp.arange(experts * capacity, dtype=jnp.int32)[:, None]
    source_row = jnp.sum(jnp.where(match, token_of_item[None, :], 0), axis=1)
    filled = jnp.any(match, axis=1)
    buffer = jnp.where(filled[:, None], group_x[source_row], jnp.zeros((), jnp.bfloat16))
    buffer = buffer.reshape(experts, capacity, group_x.shape[1])
    first = w_in[0]
    second = w_out[0]
    rows = lax.all_to_all(buffer, "expert", split_axis=0, concat_axis=0, tiled=True)
    count = rows.shape[0] * rows.shape[1]
    flat = rows.reshape(count, rows.shape[2])
    hidden = jax.nn.silu(jnp.dot(flat, first, preferred_element_type=jnp.float32)).astype(
        jnp.bfloat16
    )
    partial_value = jnp.dot(hidden, second, preferred_element_type=jnp.float32)
    partial_value = partial_value.reshape(rows.shape[0], rows.shape[1], partial_value.shape[1])
    gates_flat = group_gates.reshape(items).astype(jnp.float32)
    summed = lax.psum_scatter(
        partial_value.astype(jnp.bfloat16), "hidden", scatter_dimension=2, tiled=True
    ).astype(jnp.float32)
    back = lax.all_to_all(
        summed.astype(jnp.bfloat16), "expert", split_axis=0, concat_axis=0, tiled=True
    ).astype(summed.dtype)
    width = back.shape[2]
    picked = back.reshape(experts * capacity, width)[slot]
    mixed_part = jnp.sum((picked * gates_flat[:, None]).reshape(group, top, width), axis=1)
    result = lax.all_to_all(
        mixed_part.astype(jnp.bfloat16), "hidden", split_axis=0, concat_axis=1, tiled=True
    ).astype(mixed_part.dtype)
    return result.astype(jnp.bfloat16)


def solution(mesh):
    placed = (
        P(("expert", "hidden"), None),
        P(("expert", "hidden"), None),
        P(("expert", "hidden"), None),
        P("expert", None, "hidden"),
        P("expert", "hidden", None),
    )
    return jax.shard_map(
        per_device,
        mesh=mesh,
        in_specs=placed,
        out_specs=P(("expert", "hidden"), None),
        check_vma=False,
    )
```

profile of v0, /device:TPU:0, one launch (start us, length us, event | category | flops | bytes accessed | tf_op | source)
XLA Modules:
  0.0 143.8 jit_solution(11265905741907519250)
XLA Ops:
  6.5 5.4 %all_gather.9 = s32[16,8]{1,0:T(8,128)S(1)} all-gather(s32[8,8]{1,0:T(8,128)} %param.6), channel_id=1, replica_groups=mesh['expert'=16,'hidden'=2] {'hidden'}, dimensions={0}, use_global_device_ids=true | all-gather | bytes 768 | tf_op jit(solution)/shard_map/all_gather | solution.py:10
  12.0 0.1 reshape.102
  12.0 0.1 fusion.7
  12.1 0.2 reduce_window_sum.11
  12.3 0.2 select_reduce_fusion.1
  12.5 0.1 fusion.6
  12.6 0.1 select_reduce_fusion
  12.8 5.1 %all_gather.10 = bf16[16,3584]{1,0:T(8,128)(2,1)S(1)} all-gather(bf16[8,3584]{1,0:T(8,128)(2,1)} %param.5), channel_id=1, replica_groups=mesh['expert'=16,'hidden'=2] {'hidden'}, dimensions={0}, use_global_device_ids=true | all-gather | bytes 172032 | tf_op jit(solution)/shard_map/all_gather | solution.py:9
  17.8 0.1 broadcast_in_dim.34
  17.9 1.7 %gather_fusion = bf16[256,3584]{1,0:T(8,128)(2,1)S(1)} fusion(bf16[16,3584]{1,0:T(8,128)(2,1)S(1)} %all_gather.10, s32[1024]{0:T(1024)S(1)} %pad_clamp_fusion.1), kind=kCustom, calls=%fused_computation | custom fusion | bytes 3671040 | tf_op jit(solution)/shard_map/gather | solution.py:29
  19.7 0.2 broadcast_select_fusion
  19.9 49.2 %all_to_all.26 = bf16[16,16,3584]{2,1,0:T(8,128)(2,1)S(1)} all-to-all(bf16[16,16,3584]{2,1,0:T(8,128)(2,1)S(1)} %broadcast_select_fusion), channel_id=1, replica_groups=mesh['expert'=16,'hidden'=2] {'expert'}, dimensions={0} | all-to-all | bytes 3670016 | tf_op jit(solution)/shard_map/all_to_all | solution.py:33
  69.1 1.2 multiply_convert_fusion
  70.3 0.8 copy-done.2
  71.1 2.4 %convolution_convert_fusion = bf16[16,16,3584]{2,1,0:T(8,128)(2,1)} fusion(bf16[16,16,512]{2,1,0:T(8,128)(2,1)S(1)} %bitcast.41, bf16[1,512,3584]{2,1,0:T(8,128)(2,1)S(1)} %copy-done.2), kind=kOutput, calls=%fused_computation.2 | convolution fusion | flops 940441600 | bytes 5767168 | tf_op jit(solution)/shard_map/dot_general | solution.py:39
  73.5 28.4 %reduce-scatter.2.cloned.1.call-done = bf16[16,16,1792]{2,1,0:T(8,128)(2,1)} async-done(((bf16[16,16,3584]{2,1,0:T(8,128)(2,1)}), bf16[16,16,1792]{2,1,0:T(8,128)(2,1)}) %reduce-scatter.2.cloned.1.call-update) | async-done | bytes 917520 | tf_op jit(solution)/shard_map/reduce_scatter | solution.py:42
  102.0 5.6 %all-to-all-start.1 = ((bf16[16,16,1792]{2,1,0:T(8,128)(2,1)}), bf16[16,16,1792]{2,1,0:T(8,128)(2,1)S(1)}, u32[]{:S(2)}, u32[]{:S(2)}) async-start(bf16[16,16,1792]{2,1,0:T(8,128)(2,1)} %reduce-scatter.2.cloned.1.call-done), calls=%async_computation.2 | async-start | bytes 1835008 | tf_op jit(solution)/shard_map/all_to_all | solution.py:45
  107.7 4.3 %all_gather.11 = bf16[16,8]{1,0:T(8,128)(2,1)S(1)} all-gather(bf16[8,8]{1,0:T(8,128)(2,1)S(1)} %copy-done), channel_id=1, replica_groups=mesh['expert'=16,'hidden'=2] {'hidden'}, dimensions={0}, use_global_device_ids=true | all-gather | bytes 384 | tf_op jit(solution)/shard_map/all_gather | solution.py:11
  112.1 16.3 %all-to-all-done.1 = bf16[16,16,1792]{2,1,0:T(8,128)(2,1)S(1)} async-done(((bf16[16,16,1792]{2,1,0:T(8,128)(2,1)}), bf16[16,16,1792]{2,1,0:T(8,128)(2,1)S(1)}, u32[]{:S(2)}, u32[]{:S(2)}) %all-to-all-start.1) | async-done | bytes 917536 | tf_op jit(solution)/shard_map/all_to_all | solution.py:45
  128.4 0.2 bitcast_convert_fusion
  128.6 1.0 gather_fusion.1
  129.6 0.3 fusion.3
  129.9 6.4 %all_to_all.27 = bf16[2,8,1792]{2,1,0:T(8,128)(2,1)S(1)} all-to-all(bf16[2,8,1792]{2,1,0:T(8,128)(2,1)S(1)} %bitcast.38), channel_id=1, replica_groups=mesh['expert'=16,'hidden'=2] {'hidden'}, dimensions={0} | all-to-all | bytes 114688 | tf_op jit(solution)/shard_map/all_to_all | solution.py:51
  136.4 0.6 copy.7
  (16 shorter events, 0.2 us)
Async XLA Ops:
  6.5 95.4 %reduce-scatter.2.cloned.1.call-start = ((), (), s32[]{:S(2)}) async-start(), calls=%async_computation.4 | async-start | bytes 2752512 | tf_op jit(solution)/shard_map/reduce_scatter | solution.py:42
  19.9 49.3 %copy-start.1 = (bf16[1,3584,512]{2,1,0:T(8,128)(2,1)S(1)}, bf16[1,3584,512]{2,1,0:T(8,128)(2,1)}, u32[]{:S(2)}) copy-start(bf16[1,3584,512]{2,1,0:T(8,128)(2,1)} %param.8) | copy-start | bytes 11010052
  69.1 2.0 %copy-start.2 = (bf16[1,512,3584]{2,1,0:T(8,128)(2,1)S(1)}, bf16[1,512,3584]{2,1,0:T(8,128)(2,1)}, u32[]{:S(2)}) copy-start(bf16[1,512,3584]{2,1,0:T(8,128)(2,1)} %param.9) | copy-start | bytes 11010052
  73.5 34.2 %copy-start = (bf16[8,8]{1,0:T(8,128)(2,1)S(1)}, bf16[8,8]{1,0:T(8,128)(2,1)}, u32[]{:S(2)}) copy-start(bf16[8,8]{1,0:T(8,128)(2,1)} %param.7) | copy-start | bytes 388
  102.0 26.4 %all-to-all-start.1 = ((bf16[16,16,1792]{2,1,0:T(8,128)(2,1)}), bf16[16,16,1792]{2,1,0:T(8,128)(2,1)S(1)}, u32[]{:S(2)}, u32[]{:S(2)}) async-start(bf16[16,16,1792]{2,1,0:T(8,128)(2,1)} %reduce-scatter.2.cloned.1.call-done), calls=%async_computation.2 | async-start | bytes 1835008 | tf_op jit(solution)/shard_map/all_to_all | solution.py:45
Sparse Core Ops, SparseCore 0:
  73.7 28.2 reduce-scatter.1
where the time goes:
time: 144 us
  blocking collectives  70.5 us (49%)
  waiting for transfers between devices  44.8 us (31%)
  between operations  13.5 us (9%)
  starting transfers between devices  5.61 us (4%)
  local copies, waits for them, and re-layouts  4.43 us (3%)
  matrix products  3.57 us (2%)
    all_to_all x1, blocking collectives, per_device(): lax.all_to_all(buffer, 'expert', split_axis=0, concat_axis=0, tiled=True)  49.2 us
    reduce_scatter x1, waiting for transfers between devices, per_device(): lax.psum_scatter(partial_value.astype(jnp.bfloat16), 'hidden', scatter_di...  28.4 us
    all_to_all x1, waiting for transfers between devices, per_device(): lax.all_to_all(summed.astype(jnp.bfloat16), 'expert', split_axis=0, conca...  16.3 us
    all_to_all x1, blocking collectives, per_device(): lax.all_to_all(mixed_part.astype(jnp.bfloat16), 'hidden', split_axis=0, c...  6.45 us
    all_to_all x1, starting transfers between devices, per_device(): lax.all_to_all(summed.astype(jnp.bfloat16), 'expert', split_axis=0, conca...  5.61 us
    all_gather x1, blocking collectives, per_device(): lax.all_gather(routes, 'hidden', axis=0, tiled=True)  5.42 us
    all_gather x1, blocking collectives, per_device(): lax.all_gather(tokens, 'hidden', axis=0, tiled=True)  5.07 us
    all_gather x1, blocking collectives, per_device(): lax.all_gather(gate_weights, 'hidden', axis=0, tiled=True)  4.34 us
  transfers between devices with their start and end apart: 2, of which 2 were waited for; matrix products, arithmetic and copies ran while one was open for 0% of the time, Pallas kernels for 0%

commit v1 on v0

--- a/solution.py
+++ b/solution.py
@@ -1,10 +1,18 @@
+import functools
+
 import jax
 import jax.numpy as jnp
 from jax import lax
+from jax.experimental import pallas as pl
+from jax.experimental.pallas import tpu as pltpu
 from jax.sharding import PartitionSpec as P
 
-
-def per_device(tokens, routes, gate_weights, w_in, w_out):
+MESH = pl.DeviceIdType.MESH
+F32 = jnp.float32
+BF16 = jnp.bfloat16
+
+
+def routed_plan(tokens, routes, gate_weights, w_in, w_out):
     group_x, group_routes, group_gates = (
         lax.all_gather(tokens, "hidden", axis=0, tiled=True),
         lax.all_gather(routes, "hidden", axis=0, tiled=True),
@@ -54,7 +62,231 @@
     return result.astype(jnp.bfloat16)
 
 
+def dense_kernel(
+    zs, tok_ref, routes_ref, gates_ref, win_hbm, wout_hbm, out_ref,
+    buf_a, buf_b, win, wout, gate, act,
+    cs_a, cs_b, cr_a, cr_b, acc_a, acc_b,
+    s1_a, s1_b, r1_a, r1_b, k1_a, k1_b,
+    s2_a, s2_b, r2_a, r2_b, k2_a, k2_b,
+    s3_a, s3_b, r3_a, r3_b,
+    w_sem, gz_send, gz_recv, g_send, g_recv, r_send, r_recv, rz_send, rz_recv,
+):
+    bufs = (buf_a, buf_b)
+    cs, cr, acc = (cs_a, cs_b), (cr_a, cr_b), (acc_a, acc_b)
+    s1, r1, k1 = (s1_a, s1_b), (r1_a, r1_b), (k1_a, k1_b)
+    s2, r2, k2 = (s2_a, s2_b), (r2_a, r2_b), (k2_a, k2_b)
+    s3, r3 = (s3_a, s3_b), (r3_a, r3_b)
+    e = lax.axis_index("expert")
+    x = lax.axis_index("hidden")
+    c = lax.rem(e, 2)
+    y = lax.rem(e // 2, 2)
+    z = e // 4
+    rows, width = tok_ref.shape
+    half = width // 2
+    top = routes_ref.shape[1]
+
+    def device(zz, yy, cc, xx):
+        return ((zz * 2 + yy) * 2 + cc, xx)
+
+    x_peer = device(z, y, c, 1 - x)
+    y_peer = device(z, 1 - y, c, x)
+    c_peer = device(z, y, 1 - c, x)
+    z_peers = [device(lax.rem(z + d, zs), y, c, x) for d in range(1, zs)]
+
+    load_in = pltpu.make_async_copy(win_hbm.at[0], win, w_sem.at[0])
+    load_out = pltpu.make_async_copy(wout_hbm.at[0], wout, w_sem.at[1])
+    load_in.start()
+    load_out.start()
+
+    barrier = pltpu.get_barrier_semaphore()
+    for peer in z_peers + [x_peer, y_peer, c_peer]:
+        pl.semaphore_signal(barrier, inc=1, device_id=peer, device_id_type=MESH)
+
+    lanes = lax.broadcasted_iota(jnp.int32, (rows, 128), 1)
+    table = jnp.zeros((rows, 128), F32)
+    routes = routes_ref[...]
+    gates = gates_ref[...].astype(F32)
+    for k in range(top):
+        table = table + jnp.where(lanes == routes[:, k : k + 1], gates[:, k : k + 1], 0.0)
+    buf_a[c, x, y, z] = tok_ref[:, :half]
+    buf_b[c, x, y, z, :, :half] = tok_ref[:, half:]
+    buf_b[c, x, y, z, :, half:] = table.astype(BF16)
+
+    pl.semaphore_wait(barrier, zs + 2)
+
+    def remote(src, dst, send, recv, peer):
+        return pltpu.make_async_remote_copy(
+            src_ref=src, dst_ref=dst, send_sem=send, recv_sem=recv,
+            device_id=peer, device_id_type=MESH,
+        )
+
+    started = []
+
+    def go(copy):
+        copy.start()
+        started.append(copy)
+        return copy
+
+    for p in (0, 1):
+        for d in range(1, zs):
+            mine = bufs[p].at[c, x, y, z]
+            go(remote(mine, mine, gz_send.at[p, d], gz_recv.at[p, d], z_peers[d - 1]))
+
+    def wait_z(p):
+        for d in range(1, zs):
+            there = bufs[p].at[c, x, y, lax.rem(z + zs - d, zs)]
+            remote(there, there, gz_send.at[p, d], gz_recv.at[p, d], z_peers[d - 1]).wait_recv()
+
+    def exchange(p, stage, mine, theirs, peer):
+        go(remote(mine, mine, g_send.at[p, stage], g_recv.at[p, stage], peer))
+        return remote(theirs, theirs, g_send.at[p, stage], g_recv.at[p, stage], peer)
+
+    wait_z(0)
+    first_a = exchange(0, 0, buf_a.at[c, x, y], buf_a.at[c, x, 1 - y], y_peer)
+    wait_z(1)
+    first_b = exchange(1, 0, buf_b.at[c, x, y], buf_b.at[c, 1 - x, y], x_peer)
+    first_a.wait_recv()
+    second_a = exchange(0, 1, buf_a.at[c, x], buf_a.at[c, 1 - x], x_peer)
+    first_b.wait_recv()
+    second_b = exchange(1, 1, buf_b.at[c, :, y], buf_b.at[c, :, 1 - y], y_peer)
+    second_a.wait_recv()
+    third_a = exchange(0, 2, buf_a.at[c], buf_a.at[1 - c], c_peer)
+    second_b.wait_recv()
+    third_b = exchange(1, 2, buf_b.at[c], buf_b.at[1 - c], c_peer)
+    load_in.wait()
+
+    count = 4 * zs * rows
+
+    def flat(block):
+        return block.astype(F32).reshape(count, block.shape[-1])
+
+    def first_product(index, slot):
+        xa = flat(buf_a[index]).astype(BF16)
+        xb = flat(buf_b[index, :, :, :, :, :half]).astype(BF16)
+        h = jnp.dot(xa, win[:half, :], preferred_element_type=F32)
+        h = h + jnp.dot(xb, win[half:, :], preferred_element_type=F32)
+        act[slot] = (h / (1.0 + jnp.exp(-h))).astype(BF16)
+        tab = flat(buf_b[index, :, :, :, :, half:])
+        column = lax.broadcasted_iota(jnp.int32, tab.shape, 1)
+        g = jnp.sum(jnp.where(column == e, tab, 0.0), axis=1, keepdims=True)
+        gate[slot] = jnp.broadcast_to(g, (count, 128))
+
+    first_product(c, 0)
+    third_a.wait_recv()
+    third_b.wait_recv()
+    first_product(1 - c, 1)
+    load_out.wait()
+
+    def second_product(p, slot):
+        w = wout[:, p * half : (p + 1) * half]
+        return jnp.dot(act[slot], w, preferred_element_type=F32) * gate[slot][:, :1]
+
+    def send(p, stage, src, dst, peer):
+        return go(remote(src, dst, r_send.at[p, stage], r_recv.at[p, stage], peer))
+
+    core = []
+    for p in (0, 1):
+        value = second_product(p, 1)
+        cs[p][...] = value.reshape(cs[p].shape).astype(BF16)
+        core.append(send(p, 0, cs[p], cr[p], c_peer))
+    one = []
+    for p in (0, 1):
+        acc[p][...] = second_product(p, 0).reshape(acc[p].shape)
+    for p in (0, 1):
+        core[p].wait_recv()
+        if p == 0:
+            away = acc[p][1 - x] + cr[p][1 - x].astype(F32)
+        else:
+            away = acc[p][:, 1 - y] + cr[p][:, 1 - y].astype(F32)
+        s1[p][...] = away.astype(BF16)
+        one.append(send(p, 1, s1[p], r1[p], x_peer if p == 0 else y_peer))
+        if p == 0:
+            k1[p][...] = acc[p][x] + cr[p][x].astype(F32)
+        else:
+            k1[p][...] = acc[p][:, y] + cr[p][:, y].astype(F32)
+    two = []
+    for p in (0, 1):
+        one[p].wait_recv()
+        keep, give, peer = (y, 1 - y, y_peer) if p == 0 else (x, 1 - x, x_peer)
+        s2[p][...] = (k1[p][give] + r1[p][give].astype(F32)).astype(BF16)
+        two.append(send(p, 2, s2[p], r2[p], peer))
+        k2[p][...] = k1[p][keep] + r1[p][keep].astype(F32)
+    last = []
+    for p in (0, 1):
+        two[p].wait_recv()
+        total = k2[p][...] + r2[p][...].astype(F32)
+        k2[p][...] = total
+        s3[p][...] = total.astype(BF16)
+        for d in range(1, zs):
+            last.append(go(remote(
+                s3[p].at[lax.rem(z + d, zs)], r3[p].at[d - 1],
+                rz_send.at[p, d], rz_recv.at[p, d], z_peers[d - 1],
+            )))
+    for p in (0, 1):
+        total = k2[p][z]
+        for d in range(1, zs):
+            last[p * (zs - 1) + d - 1].wait_recv()
+            total = total + r3[p][d - 1].astype(F32)
+        out_ref[:, p * half : (p + 1) * half] = total.astype(BF16)
+    for copy in started:
+        copy.wait_send()
+
+
+def dense_plan(tokens, routes, gate_weights, w_in, w_out):
+    zs = lax.axis_size("expert") // 4
+    rows, width = tokens.shape
+    units = w_in.shape[2]
+    half = width // 2
+    count = 4 * zs * rows
+
+    def both(lead, dtype, extra=0):
+        return [pltpu.VMEM(lead + (rows, half), dtype), pltpu.VMEM(lead + (rows, half + extra), dtype)]
+
+    dma = pltpu.SemaphoreType.DMA
+    scratch = (
+        both((2, 2, 2, zs), BF16, 128)
+        + [pltpu.VMEM((width, units), BF16), pltpu.VMEM((units, width), BF16)]
+        + [pltpu.VMEM((2, count, 128), F32), pltpu.VMEM((2, count, units), BF16)]
+        + both((2, 2, zs), BF16) + both((2, 2, zs), BF16) + both((2, 2, zs), F32)
+        + both((2, zs), BF16) + both((2, zs), BF16) + both((2, zs), F32)
+        + both((zs,), BF16) + both((zs,), BF16) + both((zs,), F32)
+        + both((zs,), BF16) + both((zs - 1,), BF16)
+        + [dma((2,)), dma((2, zs)), dma((2, zs)), dma((2, 3)), dma((2, 3)),
+           dma((2, 3)), dma((2, 3)), dma((2, zs)), dma((2, zs))]
+    )
+    vmem = pl.BlockSpec(memory_space=pltpu.VMEM)
+    hbm = pl.BlockSpec(memory_space=pl.ANY)
+    return pl.pallas_call(
+        functools.partial(dense_kernel, zs),
+        out_shape=jax.ShapeDtypeStruct((rows, width), BF16),
+        in_specs=[vmem, vmem, vmem, hbm, hbm],
+        out_specs=vmem,
+        scratch_shapes=scratch,
+        compiler_params=pltpu.CompilerParams(
+            collective_id=0, has_side_effects=True, vmem_limit_bytes=48 * 2**20
+        ),
+        cost_estimate=pl.CostEstimate(
+            flops=8 * count * width * units,
+            bytes_accessed=4 * width * units,
+            transcendentals=2 * count * units,
+        ),
+    )(tokens, routes, gate_weights, w_in, w_out)
+
+
 def solution(mesh):
+    experts, parts = mesh.shape["expert"], mesh.shape["hidden"]
+
+    def per_device(tokens, routes, gate_weights, w_in, w_out):
+        group = tokens.shape[0] * parts
+        named = w_in.shape[0] * experts
+        capacity = min(group, 2 * group * routes.shape[1] // named)
+        dense = (
+            capacity == group and parts == 2 and experts % 4 == 0 and w_in.shape[0] == 1
+            and 8 <= experts <= 16 and tokens.shape[0] == 8 and tokens.shape[1] % 256 == 0
+        )
+        plan = dense_plan if dense else routed_plan
+        return plan(tokens, routes, gate_weights, w_in, w_out)
+
     placed = (
         P(("expert", "hidden"), None),
         P(("expert", "hidden"), None),

time: 144 us -> 47.5 us (0.33)
  blocking collectives: 70.5 us -> 0 us
  waiting for transfers between devices: 44.8 us -> 0 us
  Pallas kernels: 0 us -> 42.4 us
  between operations: 13.5 us -> 0.01 us
  starting transfers between devices: 5.61 us -> 0 us
  matrix products: 3.57 us -> 0 us
    all_to_all x2 -> x0, blocking collectives: 55.7 us -> none  [the longest x1 49.2 us: per_device(): lax.all_to_all(buffer, 'expert', split_axis=0, concat_axis=0, tiled=True)]
    pallas_call x0 -> x1, Pallas kernels: none -> 42.4 us  [dense_plan(): pl.pallas_call(functools.partial(dense_kernel, zs), out_shape=jax.ShapeDt...]
    reduce_scatter x1 -> x0, waiting for transfers between devices: 28.4 us -> none  [per_device(): lax.psum_scatter(partial_value.astype(jnp.bfloat16), 'hidden', scatter_di...]
    all_to_all x1 -> x0, waiting for transfers between devices: 16.3 us -> none  [per_device(): lax.all_to_all(summed.astype(jnp.bfloat16), 'expert', split_axis=0, conca...]
    all_gather x3 -> x0, blocking collectives: 14.8 us -> none  [the longest x1 5.42 us: per_device(): lax.all_gather(routes, 'hidden', axis=0, tiled=True)]
    all_to_all x1 -> x0, starting transfers between devices: 5.61 us -> none  [per_device(): lax.all_to_all(summed.astype(jnp.bfloat16), 'expert', split_axis=0, conca...]
    dot_general x2 -> x0, matrix products: 3.57 us -> none  [the longest x1 2.37 us: per_device(): partial_value = jnp.dot(hidden, second, preferred_element_type=jnp.float32)]
    unnamed x7 -> x9, local copies, waits for them, and re-layouts: 1.47 us -> 4.85 us
  transfers between devices with their start and end apart: 2 -> 0, of which waited for: 2 -> 0; matrix products, arithmetic and copies ran while one was open for 0% -> 0% of each run, Pallas kernels for 0% -> 0%
where the time goes in v1:
time: 47.5 us; the launch traced here: 47.2 us
  Pallas kernels  42.4 us (89%)
  local copies, waits for them, and re-layouts  4.85 us (10%)
    pallas_call x1, Pallas kernels, dense_plan(): pl.pallas_call(functools.partial(dense_kernel, zs), out_shape=jax.ShapeDt...  42.4 us
    unnamed x9, local copies, waits for them, and re-layouts  4.85 us

profile of v1, /device:TPU:0, one launch (start us, length us, event | category | flops | bytes accessed | tf_op | source)
XLA Modules:
  0.0 47.2 jit_solution(10374108440637461268)
XLA Ops:
  0.0 0.0 copy-start
  0.0 2.0 %copy-done = bf16[1,3584,512]{2,1,0:T(8,128)(2,1)S(1)} copy-done((bf16[1,3584,512]{2,1,0:T(8,128)(2,1)S(1)}, bf16[1,3584,512]{2,1,0:T(8,128)(2,1)}, u32[]{:S(2)}) %copy-start) | copy-done | bytes 3670040
  2.0 0.0 copy-start.1
  2.0 0.8 %copy-done.1 = bf16[8,3584]{1,0:T(8,128)(2,1)S(1)} copy-done((bf16[8,3584]{1,0:T(8,128)(2,1)S(1)}, bf16[8,3584]{1,0:T(8,128)(2,1)}, u32[]{:S(2)}) %copy-start.1) | copy-done | bytes 57368
  2.9 0.0 copy-start.2
  2.9 0.7 %copy-done.2 = s32[8,8]{1,0:T(8,128)S(1)} copy-done((s32[8,8]{1,0:T(8,128)S(1)}, s32[8,8]{1,0:T(8,128)}, u32[]{:S(2)}) %copy-start.2) | copy-done | bytes 280
  3.5 0.0 copy-start.3
  3.5 0.7 %copy-done.3 = bf16[8,8]{1,0:T(8,128)(2,1)S(1)} copy-done((bf16[8,8]{1,0:T(8,128)(2,1)S(1)}, bf16[8,8]{1,0:T(8,128)(2,1)}, u32[]{:S(2)}) %copy-start.3) | copy-done | bytes 152
  4.2 42.4 %shard_map.55 = bf16[8,3584]{1,0:T(8,128)(2,1)S(1)} custom-call(bf16[8,3584]{1,0:T(8,128)(2,1)S(1)} %copy-done.1, s32[8,8]{1,0:T(8,128)S(1)} %copy-done.2, bf16[8,8]{1,0:T(8,128)(2,1)S(1)} %copy-done.3, bf16[1,3584,512]{2,1,0:T(8,128)(2,1)S(1)} %copy-done, bf16[1,512,3584]{2,1,0:T(8,128)(2,1)} %wout_hbm.1), custom_call_target="tpu_custom_call" | custom-call | flops 1879048192 | bytes 7340032 | tf_op jit(solution)/shard_map/pallas_call | solution.py:259
  46.6 0.6 %copy.7 = bf16[8,3584]{1,0:T(8,128)(2,1)} copy(bf16[8,3584]{1,0:T(8,128)(2,1)S(1)} %shard_map.55) | data formatting | bytes 114688
Async XLA Ops:
  0.0 2.0 %copy-start = (bf16[1,3584,512]{2,1,0:T(8,128)(2,1)S(1)}, bf16[1,3584,512]{2,1,0:T(8,128)(2,1)}, u32[]{:S(2)}) copy-start(bf16[1,3584,512]{2,1,0:T(8,128)(2,1)} %win_hbm.1) | copy-start | bytes 11010052
  2.0 0.8 %copy-start.1 = (bf16[8,3584]{1,0:T(8,128)(2,1)S(1)}, bf16[8,3584]{1,0:T(8,128)(2,1)}, u32[]{:S(2)}) copy-start(bf16[8,3584]{1,0:T(8,128)(2,1)} %tok_ref.1) | copy-start | bytes 172036
  2.9 0.7 %copy-start.2 = (s32[8,8]{1,0:T(8,128)S(1)}, s32[8,8]{1,0:T(8,128)}, u32[]{:S(2)}) copy-start(s32[8,8]{1,0:T(8,128)} %routes_ref.1) | copy-start | bytes 772
  3.5 0.7 %copy-start.3 = (bf16[8,8]{1,0:T(8,128)(2,1)S(1)}, bf16[8,8]{1,0:T(8,128)(2,1)}, u32[]{:S(2)}) copy-start(bf16[8,8]{1,0:T(8,128)(2,1)} %gates_ref.1) | copy-start | bytes 388

commit v2 on v0

--- a/solution.py
+++ b/solution.py
@@ -1,10 +1,18 @@
+import functools
+
 import jax
 import jax.numpy as jnp
 from jax import lax
+from jax.experimental import pallas as pl
+from jax.experimental.pallas import tpu as pltpu
 from jax.sharding import PartitionSpec as P
 
-
-def per_device(tokens, routes, gate_weights, w_in, w_out):
+MESH = pl.DeviceIdType.MESH
+F32 = jnp.float32
+BF16 = jnp.bfloat16
+
+
+def routed_plan(tokens, routes, gate_weights, w_in, w_out):
     group_x, group_routes, group_gates = (
         lax.all_gather(tokens, "hidden", axis=0, tiled=True),
         lax.all_gather(routes, "hidden", axis=0, tiled=True),
@@ -54,7 +62,293 @@
     return result.astype(jnp.bfloat16)
 
 
+SIZES = (6, 6, 5, 5, 3, 3)
+ORDERS = (("z", "x", "y"), ("z", "y", "x"), ("z", "x", "y"), ("z", "y", "x"), ("x", "y", "z"), ("y", "x", "z"))
+FIRST = (4, 5, 1, 0, 2, 3)
+GATHER_STEPS = (
+    (4, 0), (5, 0), (4, 1), (5, 1), (1, 0), (0, 0), (2, 0), (3, 0), (0, 1), (1, 1), (2, 1), (3, 1),
+    (0, 2), (1, 2), (2, 2), (3, 2), (4, 2), (5, 2),
+)
+REDUCE_STEPS = (
+    (0, 0), (1, 0), (4, 0), (5, 0), (2, 0), (3, 0), (0, 1), (1, 1), (2, 1), (3, 1), (0, 2), (1, 2),
+    (4, 1), (5, 1), (4, 2), (5, 2), (2, 2), (3, 2),
+)
+GATE_PART = 5
+DIMS = ("x", "y", "z")
+
+
+def plan_parts(width):
+    tiles, parts, before = width // 128, [], 0
+    for size, order in zip(SIZES, ORDERS):
+        first = tiles * before // sum(SIZES)
+        before += size
+        end = tiles * before // sum(SIZES)
+        parts.append((first * 128, (end - first) * 128, order))
+    return parts
+
+
+def dense_kernel(
+    zs, parts, tok_hbm, routes_hbm, gates_hbm, win_hbm, wout_hbm, out_ref,
+    bufs, states, core_bufs, stage_bufs, routes_ref, gates_ref, win, wout, xs, gate, act,
+    w_sem, t_sem, g_send, g_recv, r_send, r_recv,
+):
+    e = lax.axis_index("expert")
+    c = lax.rem(e, 2)
+    here = {"x": lax.axis_index("hidden"), "y": lax.rem(e // 2, 2), "z": e // 4}
+    size = {"x": 2, "y": 2, "z": zs}
+    rows, width = tok_hbm.shape
+    top = routes_hbm.shape[1]
+
+    def device(at, core):
+        return ((at["z"] * 2 + at["y"]) * 2 + core, at["x"])
+
+    def moved(dim, d):
+        return lax.rem(here[dim] + d, size[dim])
+
+    def peer(dim, d):
+        return device({**here, dim: moved(dim, d)}, c)
+
+    c_peer = device(here, 1 - c)
+
+    small = [
+        pltpu.make_async_copy(routes_hbm, routes_ref, w_sem.at[2]),
+        pltpu.make_async_copy(gates_hbm, gates_ref, w_sem.at[3]),
+    ]
+    for p, (first, columns, _) in enumerate(parts):
+        small.append(pltpu.make_async_copy(
+            tok_hbm.at[:, pl.ds(first, columns)],
+            bufs[p].at[c, here["x"], here["y"], here["z"], :, pl.ds(0, columns)],
+            t_sem.at[p],
+        ))
+    for copy in small:
+        copy.start()
+    load_in = pltpu.make_async_copy(win_hbm.at[0], win, w_sem.at[0])
+    load_out = pltpu.make_async_copy(wout_hbm.at[0], wout, w_sem.at[1])
+    load_in.start()
+    load_out.start()
+
+    barrier = pltpu.get_barrier_semaphore()
+    greeted = [peer(dim, d) for dim in DIMS for d in range(1, size[dim])] + [c_peer]
+    for other in greeted:
+        pl.semaphore_signal(barrier, inc=1, device_id=other, device_id_type=MESH)
+
+    for copy in small[2:]:
+        copy.wait()
+
+    pl.semaphore_wait(barrier, len(greeted))
+
+    def remote(src, dst, send, recv, to):
+        return pltpu.make_async_remote_copy(
+            src_ref=src, dst_ref=dst, send_sem=send, recv_sem=recv,
+            device_id=to, device_id_type=MESH,
+        )
+
+    started = []
+
+    def go(copy):
+        copy.start()
+        started.append(copy)
+        return copy
+
+    def gathered(p, stage, shift):
+        order = parts[p][2]
+        index = [c]
+        for dim in DIMS:
+            if dim in order[:stage]:
+                index.append(slice(None))
+            elif dim == order[stage]:
+                index.append(moved(dim, shift))
+            else:
+                index.append(here[dim])
+        return bufs[p].at[tuple(index)]
+
+    def gather_start(p, stage):
+        if stage == 3:
+            mine = bufs[p].at[c]
+            go(remote(mine, mine, g_send.at[p, 3, 0], g_recv.at[p, 3, 0], c_peer))
+            return
+        dim = parts[p][2][stage]
+        mine = gathered(p, stage, 0)
+        for d in range(1, size[dim]):
+            go(remote(
+                mine, mine, g_send.at[p, stage, d - 1], g_recv.at[p, stage, d - 1], peer(dim, d)
+            ))
+
+    def gather_wait(p, stage):
+        if stage == 3:
+            there = bufs[p].at[1 - c]
+            remote(there, there, g_send.at[p, 3, 0], g_recv.at[p, 3, 0], c_peer).wait_recv()
+            return
+        dim = parts[p][2][stage]
+        for d in range(1, size[dim]):
+            there = gathered(p, stage, size[dim] - d)
+            remote(
+                there, there, g_send.at[p, stage, d - 1], g_recv.at[p, stage, d - 1], peer(dim, d)
+            ).wait_recv()
+
+    for p in FIRST:
+        if p != GATE_PART:
+            gather_start(p, 0)
+
+    small[0].wait()
+    small[1].wait()
+    lanes = lax.broadcasted_iota(jnp.int32, (rows, 128), 1)
+    table = jnp.zeros((rows, 128), F32)
+    routes = routes_ref[...]
+    gates = gates_ref[...].astype(F32)
+    for k in range(top):
+        table = table + jnp.where(lanes == routes[:, k : k + 1], gates[:, k : k + 1], 0.0)
+    own = (c, here["x"], here["y"], here["z"])
+    tail = parts[GATE_PART][1]
+    bufs[GATE_PART][own + (slice(None), slice(tail, tail + 128))] = table.astype(BF16)
+    gather_start(GATE_PART, 0)
+    for p, stage in GATHER_STEPS:
+        gather_wait(p, stage)
+        gather_start(p, stage + 1)
+    load_in.wait()
+
+    count = 4 * zs * rows
+
+    def flat(block):
+        return block.astype(F32).reshape(count, block.shape[-1])
+
+    def first_product(half, slot):
+        for p, (first, columns, _) in enumerate(parts):
+            block = bufs[p][half, :, :, :, :, :columns]
+            xs[:, first : first + columns] = flat(block).astype(BF16)
+        h = jnp.dot(xs[...], win[...], preferred_element_type=F32)
+        act[slot] = (h / (1.0 + jnp.exp(-h))).astype(BF16)
+        tab = flat(bufs[GATE_PART][half, :, :, :, :, tail : tail + 128])
+        column = lax.broadcasted_iota(jnp.int32, tab.shape, 1)
+        g = jnp.sum(jnp.where(column == e, tab, 0.0), axis=1, keepdims=True)
+        gate[slot] = jnp.broadcast_to(g, (count, 128))
+
+    first_product(c, 0)
+    for p in range(len(parts)):
+        gather_wait(p, 3)
+    first_product(1 - c, 1)
+    load_out.wait()
+
+    def second_product(p, slot):
+        first, columns, _ = parts[p]
+        w = wout[:, first : first + columns]
+        return jnp.dot(act[slot], w, preferred_element_type=F32) * gate[slot][:, :1]
+
+    arriving = {}
+    for p in range(len(parts)):
+        give, take = core_bufs[p]
+        give[...] = second_product(p, 1).reshape(give.shape).astype(BF16)
+        arriving[p] = [(go(remote(give, take, r_send.at[p, 3, 0], r_recv.at[p, 3, 0], c_peer)), take)]
+
+    def reduce_step(p, stage):
+        order = parts[p][2][::-1]
+        dim = order[stage]
+        left = [d for d in DIMS if d not in order[:stage]]
+        if stage == 0:
+            states[p][0][...] = second_product(p, 0).reshape(states[p][0].shape)
+        for copy, _ in arriving[p]:
+            copy.wait_recv()
+        coming = [ref for _, ref in arriving[p]]
+
+        def take(shift):
+            index = tuple(moved(d, shift) if d == dim else slice(None) for d in left)
+            total = states[p][stage][index]
+            for ref in coming:
+                total = total + ref[index].astype(F32)
+            return total
+
+        give, room = stage_bufs[p][stage]
+        sent = []
+        for d in range(1, size[dim]):
+            give[d - 1] = take(d).astype(BF16)
+            sent.append((go(remote(
+                give.at[d - 1], room.at[d - 1],
+                r_send.at[p, stage, d - 1], r_recv.at[p, stage, d - 1], peer(dim, d),
+            )), room.at[d - 1]))
+        states[p][stage + 1][...] = take(0)
+        arriving[p] = sent
+
+    for p, stage in REDUCE_STEPS:
+        reduce_step(p, stage)
+    for p, (first, columns, _) in enumerate(parts):
+        total = states[p][3][...]
+        for copy, ref in arriving[p]:
+            copy.wait_recv()
+            total = total + ref[...].astype(F32)
+        out_ref[:, first : first + columns] = total.astype(BF16)
+    for copy in started:
+        copy.wait_send()
+
+
+def dense_plan(tokens, routes, gate_weights, w_in, w_out):
+    zs = lax.axis_size("expert") // 4
+    rows, width = tokens.shape
+    units = w_in.shape[2]
+    count = 4 * zs * rows
+    size = {"x": 2, "y": 2, "z": zs}
+    parts = plan_parts(width)
+    dma = pltpu.SemaphoreType.DMA
+
+    bufs, states, core_bufs, stage_bufs = [], [], [], []
+    for p, (_, columns, order) in enumerate(parts):
+        extra = 128 if p == GATE_PART else 0
+        bufs.append(pltpu.VMEM((2, 2, 2, zs, rows, columns + extra), BF16))
+        left = list(DIMS)
+
+        def shape(lead=()):
+            return lead + tuple(size[d] for d in left) + (rows, columns)
+
+        core_bufs.append((pltpu.VMEM(shape(), BF16), pltpu.VMEM(shape(), BF16)))
+        state, stages = [pltpu.VMEM(shape(), F32)], []
+        for dim in order[::-1]:
+            left.remove(dim)
+            lead = (size[dim] - 1,)
+            stages.append((pltpu.VMEM(shape(lead), BF16), pltpu.VMEM(shape(lead), BF16)))
+            state.append(pltpu.VMEM(shape(), F32))
+        states.append(tuple(state))
+        stage_bufs.append(tuple(stages))
+    n = len(parts)
+    scratch = (
+        tuple(bufs), tuple(states), tuple(core_bufs), tuple(stage_bufs),
+        pltpu.VMEM(routes.shape, routes.dtype), pltpu.VMEM(gate_weights.shape, BF16),
+        pltpu.VMEM((width, units), BF16), pltpu.VMEM((units, width), BF16),
+        pltpu.VMEM((count, width), BF16),
+        pltpu.VMEM((2, count, 128), F32), pltpu.VMEM((2, count, units), BF16),
+        dma((4,)), dma((n,)),
+        dma((n, 4, zs - 1)), dma((n, 4, zs - 1)), dma((n, 4, zs - 1)), dma((n, 4, zs - 1)),
+    )
+    hbm = pl.BlockSpec(memory_space=pltpu.HBM)
+    return pl.pallas_call(
+        functools.partial(dense_kernel, zs, parts),
+        out_shape=jax.ShapeDtypeStruct((rows, width), BF16),
+        in_specs=[hbm] * 5,
+        out_specs=pl.BlockSpec(memory_space=pltpu.VMEM),
+        scratch_shapes=scratch,
+        compiler_params=pltpu.CompilerParams(
+            collective_id=0, has_side_effects=True, vmem_limit_bytes=64 * 2**20
+        ),
+        cost_estimate=pl.CostEstimate(
+            flops=8 * count * width * units,
+            bytes_accessed=4 * width * units,
+            transcendentals=2 * count * units,
+        ),
+    )(tokens, routes, gate_weights, w_in, w_out)
+
+
 def solution(mesh):
+    experts, parts = mesh.shape["expert"], mesh.shape["hidden"]
+
+    def per_device(tokens, routes, gate_weights, w_in, w_out):
+        group = tokens.shape[0] * parts
+        named = w_in.shape[0] * experts
+        capacity = min(group, 2 * group * routes.shape[1] // named)
+        dense = (
+            capacity == group and parts == 2 and experts % 4 == 0 and w_in.shape[0] == 1
+            and 8 <= experts <= 16 and tokens.shape[0] == 8 and tokens.shape[1] % 128 == 0 and tokens.shape[1] >= 1024
+        )
+        plan = dense_plan if dense else routed_plan
+        return plan(tokens, routes, gate_weights, w_in, w_out)
+
     placed = (
         P(("expert", "hidden"), None),
         P(("expert", "hidden"), None),

time: 144 us -> 43 us (0.30)
  blocking collectives: 70.5 us -> 0 us
  waiting for transfers between devices: 44.8 us -> 0 us
  Pallas kernels: 0 us -> 41.4 us
  between operations: 13.5 us -> 0.01 us
  starting transfers between devices: 5.61 us -> 0 us
  matrix products: 3.57 us -> 0 us
  local copies, waits for them, and re-layouts: 4.43 us -> 1.45 us
    all_to_all x2 -> x0, blocking collectives: 55.7 us -> none  [the longest x1 49.2 us: per_device(): lax.all_to_all(buffer, 'expert', split_axis=0, concat_axis=0, tiled=True)]
    pallas_call x0 -> x1, Pallas kernels: none -> 41.4 us  [dense_plan(): pl.pallas_call(functools.partial(dense_kernel, zs, parts), out_shape=jax....]
    reduce_scatter x1 -> x0, waiting for transfers between devices: 28.4 us -> none  [per_device(): lax.psum_scatter(partial_value.astype(jnp.bfloat16), 'hidden', scatter_di...]
    all_to_all x1 -> x0, waiting for transfers between devices: 16.3 us -> none  [per_device(): lax.all_to_all(summed.astype(jnp.bfloat16), 'expert', split_axis=0, conca...]
    all_gather x3 -> x0, blocking collectives: 14.8 us -> none  [the longest x1 5.42 us: per_device(): lax.all_gather(routes, 'hidden', axis=0, tiled=True)]
    all_to_all x1 -> x0, starting transfers between devices: 5.61 us -> none  [per_device(): lax.all_to_all(summed.astype(jnp.bfloat16), 'expert', split_axis=0, conca...]
    dot_general x2 -> x0, matrix products: 3.57 us -> none  [the longest x1 2.37 us: per_device(): partial_value = jnp.dot(hidden, second, preferred_element_type=jnp.float32)]
    gather x2 -> x0, local copies, waits for them, and re-layouts: 2.7 us -> none  [the longest x1 1.72 us: per_device(): group_x[source_row]]
  transfers between devices with their start and end apart: 2 -> 0, of which waited for: 2 -> 0; matrix products, arithmetic and copies ran while one was open for 0% -> 0% of each run, Pallas kernels for 0% -> 0%
where the time goes in v2:
time: 43 us; the launch traced here: 42.9 us
  Pallas kernels  41.4 us (96%)
  local copies, waits for them, and re-layouts  1.45 us (3%)
    pallas_call x1, Pallas kernels, dense_plan(): pl.pallas_call(functools.partial(dense_kernel, zs, parts), out_shape=jax....  41.4 us
    unnamed x1, local copies, waits for them, and re-layouts  1.45 us

profile of v2, /device:TPU:0, one launch (start us, length us, event | category | flops | bytes accessed | tf_op | source)
XLA Modules:
  0.0 42.9 jit_solution(3645125709647401860)
XLA Ops:
  0.0 41.4 %shard_map.55 = bf16[8,3584]{1,0:T(8,128)(2,1)} custom-call(bf16[8,3584]{1,0:T(8,128)(2,1)} %tok_hbm.1, s32[8,8]{1,0:T(8,128)} %routes_hbm.1, bf16[8,8]{1,0:T(8,128)(2,1)} %gates_hbm.1, bf16[1,3584,512]{2,1,0:T(8,128)(2,1)} %win_hbm.1, bf16[1,512,3584]{2,1,0:T(8,128)(2,1)} %wout_hbm.1), custom_call_target="tpu_custom_call" | custom-call | flops 1879048192 | bytes 7340032 | tf_op jit(solution)/shard_map/pallas_call | solution.py:321
  41.4 1.4 %copy.7 = bf16[8,3584]{1,0:T(8,128)(2,1)} copy(bf16[8,3584]{1,0:T(8,128)(2,1)} %shard_map.55) | data formatting | bytes 114688

commit v3 on v2

--- a/solution.py
+++ b/solution.py
@@ -64,9 +64,9 @@
 
 SIZES = (6, 6, 5, 5, 3, 3)
 ORDERS = (("z", "x", "y"), ("z", "y", "x"), ("z", "x", "y"), ("z", "y", "x"), ("x", "y", "z"), ("y", "x", "z"))
-FIRST = (4, 5, 1, 0, 2, 3)
+FIRST = (0, 1, 4, 2, 3, 5)
 GATHER_STEPS = (
-    (4, 0), (5, 0), (4, 1), (5, 1), (1, 0), (0, 0), (2, 0), (3, 0), (0, 1), (1, 1), (2, 1), (3, 1),
+    (4, 0), (5, 0), (0, 0), (1, 0), (2, 0), (3, 0), (4, 1), (5, 1), (0, 1), (1, 1), (2, 1), (3, 1),
     (0, 2), (1, 2), (2, 2), (3, 2), (4, 2), (5, 2),
 )
 REDUCE_STEPS = (

time: 43 us -> 41.9 us (0.974)
  Pallas kernels: 41.4 us -> 40.3 us
    pallas_call x1, Pallas kernels: 41.4 us -> 40.3 us  [dense_plan(): pl.pallas_call(functools.partial(dense_kernel, zs, parts), out_shape=jax....]
where the time goes in v3:
time: 41.9 us; the launch traced here: 41.8 us
  Pallas kernels  40.3 us (96%)
  local copies, waits for them, and re-layouts  1.45 us (3%)
    pallas_call x1, Pallas kernels, dense_plan(): pl.pallas_call(functools.partial(dense_kernel, zs, parts), out_shape=jax....  40.3 us
    unnamed x1, local copies, waits for them, and re-layouts  1.45 us

profile of v3, /device:TPU:0, one launch (start us, length us, event | category | flops | bytes accessed | tf_op | source)
XLA Modules:
  0.0 41.8 jit_solution(2010863082230804659)
XLA Ops:
  0.0 40.3 %shard_map.55 = bf16[8,3584]{1,0:T(8,128)(2,1)} custom-call(bf16[8,3584]{1,0:T(8,128)(2,1)} %tok_hbm.1, s32[8,8]{1,0:T(8,128)} %routes_hbm.1, bf16[8,8]{1,0:T(8,128)(2,1)} %gates_hbm.1, bf16[1,3584,512]{2,1,0:T(8,128)(2,1)} %win_hbm.1, bf16[1,512,3584]{2,1,0:T(8,128)(2,1)} %wout_hbm.1), custom_call_target="tpu_custom_call" | custom-call | flops 1879048192 | bytes 7340032 | tf_op jit(solution)/shard_map/pallas_call | solution.py:321
  40.3 1.4 %copy.7 = bf16[8,3584]{1,0:T(8,128)(2,1)} copy(bf16[8,3584]{1,0:T(8,128)(2,1)} %shard_map.55) | data formatting | bytes 114688
